TPU v7x, 32 devices: a whole 2x2x4 slice. The times are simulated.
32 devices in a mesh: groups: 2 (over y), dp: 4 (over z), tensor: 4 (over x, core).
Axes of the slice: x: 2, y: 2, z: 4, core: 2. Of those that a mesh axis runs over, the one named last changes fastest.
Arguments:
- hidden_rows: bfloat16 [4096, 3, 8192], P(('groups', 'dp'), None, 'tensor'), parts along dimension 0, may hold values from -120 to 120
- layer_gain: float32 [3, 8192], P(None, 'tensor'), may hold values from 0.1 to 1.9
- key_weight: bfloat16 [8192, 1024], P(('tensor', 'dp')), may hold values from -0.0625 to 0.0625
- step_decay: float32 [1024], P('tensor'), may hold values from 0.3 to 1
- owner_list: int32 [256], P('groups'), parts along dimension 0, may hold values from 0 to 3, as said below
- segment_len: int32 [256], P('groups'), parts along dimension 0, may hold values from 1 to 16
- reweight_count: int32 [256], P('groups'), parts along dimension 0, may hold values from 1 to 4
- loss_mask: int32 [4096], P('groups'), parts along dimension 0, may hold values 0 or 1
- state_cotangent: bfloat16 [3, 256, 16, 1024], P(None, ('groups', 'dp'), None, 'tensor'), parts along dimension 1, may hold values from -0.125 to 0.125
Outputs:
- states: bfloat16 [3, 256, 16, 1024], P(None, ('groups', 'dp'), None, 'tensor'), parts along dimension 1
- weight_grad: float32 [16384, 1024], P(('groups', 'tensor', 'dp')), parts along dimension 0
There are 2 independent parts, one for each index of `groups`. A program takes and returns all parts, laid end to end along the dimension named above; an argument that names none is the same for every part. Nothing has to cross between parts.
Inputs may be any that keep to these rules, and one draw needn't show every extreme that they name: `owner_list`: every owner receives exactly 32 segments in all; at most 16 segments of one index of dp share an owner, and exactly 16 for some pair in every draw.
All inputs are finite; a program needn't handle non-finite values.
Results may differ from a plain program's by a relative error of at most 0.0049.
Values may be sent and summed in bfloat16 or wider, within the bound.
A program may use at most 128 MiB of HBM per device.

v0:
```python
import jax
import jax.numpy as jnp
from jax import lax
from jax.sharding import PartitionSpec as P

D = 8192
SEG = 16
SEG_DEV = 32


epsilon = 1e-05


def shift_down(values):
    zeros = jnp.zeros_like(values[:, :1])
    return jnp.concatenate([zeros, values[:, :-1]], axis=1)


def shift_up(values):
    zeros = jnp.zeros_like(values[:, :1])
    return jnp.concatenate([values[:, 1:], zeros], axis=1)


def unrolled_steps(key_rows, decay_part):
    second = key_rows + decay_part * shift_down(key_rows)
    third = key_rows + decay_part * shift_down(second)
    return jnp.stack([key_rows, second, third])


def unrolled_grads(state_grads, decay_part):
    grad_third = state_grads[2]
    grad_second = state_grads[1] + decay_part * shift_up(grad_third)
    grad_first = state_grads[0] + decay_part * shift_up(grad_second)
    return grad_first + grad_second + grad_third


def layer_squares(row_block):
    values = row_block.astype(jnp.float32)
    return jnp.sum(values * values, axis=-1)


def normalize(row_block, squares, live_mask, layer_gain):
    inverse = lax.rsqrt(squares / D + epsilon)
    mixture = jnp.sum(row_block.astype(jnp.float32) * layer_gain * inverse[..., None], axis=2)
    return (mixture * live_mask[..., None]).astype(jnp.bfloat16)


def per_device(
    hidden_rows,
    layer_gain,
    key_weight,
    step_decay,
    owner_list,
    segment_len,
    reweight_count,
    loss_mask,
    state_cotangent,
):
    dp_count = lax.axis_size("dp")
    dp_index = lax.axis_index("dp")
    tp_index = lax.axis_index("tensor")
    part_width = hidden_rows.shape[2]
    key_width = key_weight.shape[1]
    share_width = state_cotangent.shape[3]
    capacity = max(2, (2 * SEG_DEV + dp_count - 1) // dp_count)
    slot_total = dp_count * capacity
    owner_table = owner_list.reshape(dp_count, SEG_DEV)
    positions = jnp.arange(SEG)
    segment_ids = jnp.arange(dp_count * SEG_DEV)
    local_ids = jnp.arange(SEG_DEV)
    slot_ids = jnp.arange(slot_total)
    zero_value = jnp.zeros((), jnp.bfloat16)
    my_owners = lax.dynamic_index_in_dim(owner_table, dp_index, 0, keepdims=False)
    earlier = (my_owners[None, :] == my_owners[:, None]) & (local_ids[None, :] < local_ids[:, None])
    slot_out = my_owners * capacity + jnp.sum(earlier, axis=1)
    out_match = slot_ids[:, None] == slot_out[None, :]
    send_pick = jnp.sum(jnp.where(out_match, local_ids[None, :], 0), axis=1)
    send_used = jnp.any(out_match, axis=1)
    incoming = owner_table == dp_index
    flat_in = incoming.reshape(-1)
    rank_flat = jnp.cumsum(flat_in.astype(jnp.int32)) - 1
    within_src = (jnp.cumsum(incoming.astype(jnp.int32), axis=1) - 1).reshape(-1)
    chosen = (rank_flat[None, :] == local_ids[:, None]) & flat_in[None, :]
    global_seg = jnp.sum(jnp.where(chosen, segment_ids[None, :], 0), axis=1)
    slot_in = jnp.sum(
        jnp.where(chosen, (segment_ids // SEG_DEV * capacity + within_src)[None, :], 0), axis=1
    )
    live_owner = (positions[None, :] < segment_len[global_seg][:, None]).astype(jnp.float32)
    mask_table = loss_mask.reshape(dp_count * SEG_DEV, SEG).astype(jnp.float32)
    weight_table = reweight_count.astype(jnp.float32)
    scale_owner = mask_table[global_seg] * weight_table[global_seg][:, None]
    row_block = hidden_rows.reshape(SEG_DEV, SEG, hidden_rows.shape[1], part_width)
    outgoing = jnp.where(send_used[:, None, None, None], row_block[send_pick], zero_value)
    arrived = lax.all_to_all(outgoing, "dp", split_axis=0, concat_axis=0, tiled=True)
    owner_rows = arrived[slot_in]
    squares = lax.psum(layer_squares(owner_rows), "tensor")
    joined_rows = normalize(owner_rows, squares, live_owner, layer_gain)
    flat_rows = joined_rows.reshape(-1, part_width)
    columns = flat_rows
    partial_keys = jnp.dot(
        columns,
        lax.all_gather(key_weight, "dp", axis=0, tiled=True),
        preferred_element_type=jnp.float32,
    )
    summed_keys = lax.psum(partial_keys, "tensor")
    key_share = lax.dynamic_slice_in_dim(summed_keys, tp_index * share_width, share_width, 1)
    states = unrolled_steps(key_share.reshape(SEG_DEV, SEG, share_width), step_decay).astype(
        jnp.bfloat16
    )
    state_grads = state_cotangent.astype(jnp.float32) * scale_owner[None, :, :, None]
    key_grads = unrolled_grads(state_grads, step_decay).astype(jnp.bfloat16)
    all_grads = lax.all_gather(key_grads, "tensor", axis=2, tiled=True)
    flat_grads = all_grads.reshape(-1, key_width)
    weight_flat_rows = joined_rows.reshape(-1, part_width)
    columns = weight_flat_rows
    weight_grad = lax.psum_scatter(
        lax.dot_general(
            columns, flat_grads, (((0,), (0,)), ((), ())), preferred_element_type=jnp.float32
        ),
        "dp",
        scatter_dimension=0,
        tiled=True,
    )
    return (states, weight_grad)


def solution(mesh):
    return jax.shard_map(
        per_device,
        mesh=mesh,
        in_specs=(
            P(("groups", "dp"), None, "tensor"),
            P(None, "tensor"),
            P(("tensor", "dp"), None),
            P("tensor"),
            P("groups"),
            P("groups"),
            P("groups"),
            P("groups"),
            P(None, ("groups", "dp"), None, "tensor"),
        ),
        out_specs=(P(None, ("groups", "dp"), None, "tensor"), P(("groups", "tensor", "dp"), None)),
        check_vma=False,
    )
```

profile of v0, /device:TPU:9, one launch (start us, length us, event | category | flops | bytes accessed | tf_op | source)
XLA Modules:
  0.0 641.6 jit_solution(13709205642636107498)
XLA Ops:
  7.2 0.7 reshape.166
  7.9 0.2 convert_reduce_fusion
  8.3 9.8 %gather_fusion = bf16[64,16,3,2048]{3,1,2,0:T(8,128)(2,1)} fusion(bf16[32,16,3,2048]{3,1,0,2:T(8,128)(2,1)} %bitcast.58, s32[1024]{0:T(1024)S(1)} %pad_clamp_fusion.2), kind=kCustom, calls=%fused_computation | custom fusion | bytes 25166080 | tf_op jit(solution)/shard_map/gather | solution.py:93
  18.2 10.8 %broadcast_select_fusion = bf16[64,16,3,2048]{3,1,2,0:T(8,128)(2,1)} fusion(bf16[64,16,3,2048]{3,1,2,0:T(8,128)(2,1)} %gather_fusion, pred[64]{0:T(512)(128)(4,1)S(1)} %fusion.11), kind=kLoop, calls=%fused_computation.10 | loop fusion | flops 6291456 | bytes 25165888 | tf_op jit(solution)/shard_map/jit(_where)/select_n | solution.py:93
  28.9 6.5 %all-to-all-start = ((bf16[64,16,3,2048]{3,1,2,0:T(8,128)(2,1)}), bf16[64,16,3,2048]{3,1,2,0:T(8,128)(2,1)}, u32[]{:S(2)}, u32[]{:S(2)}) async-start(bf16[64,16,3,2048]{3,1,2,0:T(8,128)(2,1)} %broadcast_select_fusion), calls=%async_computation | async-start | bytes 25165824 | tf_op jit(solution)/shard_map/all_to_all | solution.py:94
  35.5 0.7 all-gather.3.cloned.1.call-update
  36.2 0.2 reduce_window_sum.18
  36.5 0.1 copy.28
  36.7 0.2 reduce-window.8
  36.8 0.1 add_reduce_fusion
  36.9 0.1 select_reduce_fusion
  37.1 0.7 gather_fusion.2
  38.0 334.5 %all-to-all-done = bf16[64,16,3,2048]{3,1,2,0:T(8,128)(2,1)} async-done(((bf16[64,16,3,2048]{3,1,2,0:T(8,128)(2,1)}), bf16[64,16,3,2048]{3,1,2,0:T(8,128)(2,1)}, u32[]{:S(2)}, u32[]{:S(2)}) %all-to-all-start) | async-done | bytes 12582944 | tf_op jit(solution)/shard_map/all_to_all | solution.py:94
  372.5 8.1 %gather_fusion.1 = bf16[32,16,3,2048]{3,1,2,0:T(8,128)(2,1)} fusion(bf16[64,16,3,2048]{3,1,2,0:T(8,128)(2,1)} %all-to-all-done, s32[1024]{0:T(1024)S(1)} %pad_clamp_fusion.1), kind=kCustom, calls=%fused_computation.1 | custom fusion | bytes 12583040 | tf_op jit(solution)/shard_map/gather | solution.py:95
  380.6 4.1 fusion.2
  384.8 11.1 %psum.14 = f32[32,16,3]{0,1,2:T(8,128)S(1)} all-reduce(f32[32,16,3]{0,1,2:T(8,128)S(1)} %copy.29), channel_id=1, replica_groups=mesh['groups'=2,'dp'=4,'tensor'=4] {'tensor'}, use_global_device_ids=true, to_apply=%region_7.8 | all-reduce | flops 1536 | bytes 12288 | tf_op jit(solution)/shard_map/psum | solution.py:96
  396.0 5.1 fusion.1
  401.1 2.0 copy-done.2
  403.1 0.3 fusion.3
  403.4 5.9 fusion.23
  409.6 0.6 gather_fusion.3
  410.2 0.7 gather_fusion.4
  410.9 0.2 convert_multiply_fusion.2
  411.3 51.5 %all-reduce.6.cloned.1.call-done = f32[512,1024]{1,0:T(8,128)} async-done(((f32[512,1024]{1,0:T(8,128)}), f32[512,1024]{1,0:T(8,128)}) %all-reduce.6.cloned.1.call-update) | async-done | bytes 2097168 | tf_op jit(solution)/shard_map/psum | solution.py:105
  462.8 1.1 fusion.22
  463.9 0.3 convert_bitcast_fusion
  464.2 1.1 fusion.9
  465.3 0.2 reduce-scatter.2.cloned.1.call-start
  465.5 17.3 %all-gather.5.cloned.1.call-done = bf16[32,16,1024]{2,1,0:T(8,128)(2,1)} async-done(((bf16[32,16,256]{2,1,0:T(8,128)(2,1)}), bf16[32,16,1024]{2,1,0:T(8,128)(2,1)}) %all-gather.5.cloned.1.call-update) | async-done | bytes 1048592 | tf_op jit(solution)/shard_map/all_gather | solution.py:112
  482.9 8.2 %convolution_bitcast_fusion = f32[2048,1024]{1,0:T(8,128)} fusion(bf16[32,16,1024]{2,1,0:T(8,128)(2,1)} %all-gather.5.cloned.1.call-done, f32[32,16,2048]{2,1,0:T(8,128)} %copy-done.2, f32[32,16]{1,0:T(8,128)S(1)} %fusion.14), kind=kOutput, calls=%fused_computation.11 | convolution fusion | flops 2149580800 | bytes 13633536 | tf_op jit(solution)/shard_map/dot_general | solution.py:117
  491.1 1.0 pad_maximum_fusion
  492.1 143.0 %reduce-scatter.2.cloned.1.call-done = f32[512,1024]{1,0:T(8,128)} async-done(((f32[2048,1024]{1,0:T(8,128)}), f32[512,1024]{1,0:T(8,128)}) %reduce-scatter.2.cloned.1.call-update) | async-done | bytes 2097168 | tf_op jit(solution)/shard_map/reduce_scatter | solution.py:116
  (51 shorter events, 1.2 us)
Async XLA Ops:
  7.2 29.9 %copy-start = (s32[128]{0:T(128)S(1)}, s32[128]{0:T(128)}, u32[]{:S(2)}) copy-start(s32[128]{0:T(128)} %param.14) | copy-start | bytes 1540
  28.9 7.6 %copy-start.7 = (s32[128]{0:T(128)S(1)}, s32[128]{0:T(128)}, u32[]{:S(2)}) copy-start(s32[128]{0:T(128)} %param.13) | copy-start | bytes 1540
  28.9 343.5 %all-to-all-start = ((bf16[64,16,3,2048]{3,1,2,0:T(8,128)(2,1)}), bf16[64,16,3,2048]{3,1,2,0:T(8,128)(2,1)}, u32[]{:S(2)}, u32[]{:S(2)}) async-start(bf16[64,16,3,2048]{3,1,2,0:T(8,128)(2,1)} %broadcast_select_fusion), calls=%async_computation | async-start | bytes 25165824 | tf_op jit(solution)/shard_map/all_to_all | solution.py:94
  35.4 368.0 %all-gather.3.cloned.1.call-start = ((), (), s32[]{:S(2)}) async-start(), calls=%async_computation.2 | async-start | bytes 5242880 | tf_op jit(solution)/shard_map/all_gather | solution.py:102
  36.2 426.6 %all-reduce.6.cloned.1.call-start = ((), (), s32[]{:S(2)}) async-start(), calls=%async_computation.3 | async-start | bytes 4194304 | tf_op jit(solution)/shard_map/psum | solution.py:105
  380.6 15.4 %copy-start.4 = (f32[3,2048]{1,0:T(4,128)S(1)}, f32[3,2048]{1,0:T(4,128)}, u32[]{:S(2)}) copy-start(f32[3,2048]{1,0:T(4,128)} %param.10) | copy-start | bytes 73732
  401.1 2.0 copy-start.2
  403.4 6.1 copy-start.5
  403.4 6.8 %copy-start.8 = (s32[128]{0:T(128)S(1)}, s32[128]{0:T(128)}, u32[]{:S(2)}) copy-start(s32[128]{0:T(128)} %param.15) | copy-start | bytes 1540
  403.4 7.5 %copy-start.3 = (bf16[3,32,16,256]{3,2,1,0:T(8,128)(2,1)S(1)}, bf16[3,32,16,256]{3,2,1,0:T(8,128)(2,1)}, u32[]{:S(2)}) copy-start(bf16[3,32,16,256]{3,2,1,0:T(8,128)(2,1)} %param.17) | copy-start | bytes 2359300
  409.4 54.5 %copy-start.6 = (f32[256]{0:T(256)S(1)}, f32[256]{0:T(256)}, u32[]{:S(2)}) copy-start(f32[256]{0:T(256)} %param.12) | copy-start | bytes 3076
  409.4 73.5 %all-gather.5.cloned.1.call-start = ((), (), s32[]{:S(2)}) async-start(), calls=%async_computation.4 | async-start | bytes 1310720 | tf_op jit(solution)/shard_map/all_gather | solution.py:112
  465.3 169.7 %reduce-scatter.2.cloned.1.call-start = ((), (), s32[]{:S(2)}) async-start(), calls=%async_computation.5 | async-start | bytes 10485760 | tf_op jit(solution)/shard_map/reduce_scatter | solution.py:116
  491.1 144.0 %copy-start.1 = (s32[128]{0:T(128)S(1)}, s32[128]{0:T(128)}, u32[]{:S(2)}) copy-start(s32[128]{0:T(128)} %param.14) | copy-start | bytes 1540
Sparse Core Ops, SparseCore 0:
  37.8 168.0 all-gather.2
  409.5 53.1 all-reduce.5
  465.4 17.3 all-gather.4
  491.2 143.7 reduce-scatter.1
where the time goes:
time: 644 us; the launch traced here: 642 us
  waiting for transfers between devices  547 us (85%)
  other arithmetic  25.1 us (4%)
  local copies, waits for them, and re-layouts  23.3 us (4%)
  matrix products  14.1 us (2%)
  between operations  14 us (2%)
  blocking collectives  11.1 us (2%)
  starting transfers between devices  6.83 us (1%)
    all_to_all x1, waiting for transfers between devices, per_device(): lax.all_to_all(outgoing, 'dp', split_axis=0, concat_axis=0, tiled=True)  334 us
    reduce_scatter x1, waiting for transfers between devices, per_device(): lax.psum_scatter(lax.dot_general(columns, flat_grads, (((0,), (0,)), ((),...  143 us
    psum x1, waiting for transfers between devices, per_device(): summed_keys = lax.psum(partial_keys, 'tensor')  51.5 us
    all_gather x1, waiting for transfers between devices, per_device(): all_grads = lax.all_gather(key_grads, 'tensor', axis=2, tiled=True)  17.3 us
  transfers between devices with their start and end apart: 5, of which 4 were waited for; matrix products, arithmetic and copies ran while one was open for 3% of the time, Pallas kernels for 0%

commit v1 on v0

--- a/solution.py
+++ b/solution.py
@@ -1,6 +1,8 @@
 import jax
 import jax.numpy as jnp
 from jax import lax
+from jax.experimental import pallas as pl
+from jax.experimental.pallas import tpu as pltpu
 from jax.sharding import PartitionSpec as P
 
 D = 8192
@@ -124,9 +126,494 @@
     return (states, weight_grad)
 
 
+N_DP = 4
+N_TP = 4
+CHUNK = 128
+BF16 = jnp.bfloat16
+F32 = jnp.float32
+
+
+def fused_kernel(
+    dest_ref,
+    hidden_ref,
+    gain_ref,
+    live_ref,
+    weight_ref,
+    decay_ref,
+    grads_ref,
+    states_ref,
+    wgrad_ref,
+    hid,
+    sqcol,
+    sqsend,
+    sqrecv,
+    invcol,
+    jloc,
+    jfeat,
+    jown,
+    jturn,
+    order,
+    gbuf,
+    psend,
+    precv,
+    pown,
+    xsend,
+    xrecv,
+    keys,
+    keysb,
+    ksend,
+    krecv,
+    hid_sem,
+    sq_ss,
+    sq_rs,
+    j_ss,
+    j_rs,
+    gz_ss,
+    gz_rs,
+    gx_ss,
+    gx_rs,
+    gc_ss,
+    gc_rs,
+    kc_ss,
+    kc_rs,
+    kx_ss,
+    kx_rs,
+    kz_ss,
+    kz_rs,
+):
+    z = lax.axis_index("dp")
+    t = lax.axis_index("tensor")
+    x = t // 2
+    c = t % 2
+    t_x = (t + 2) % N_TP
+    t_c = t + 1 - 2 * c
+    t_xc = (t_c + 2) % N_TP
+    tokens = hid.shape[1]
+    feats = weight_ref.shape[0]
+    share = grads_ref.shape[1]
+    n_chunk = tokens // CHUNK
+
+    def zto(k):
+        return (z + k) % N_DP
+
+    def zfrom(k):
+        return (z + N_DP - k) % N_DP
+
+    def lanes(index, width):
+        return pl.ds(pl.multiple_of(index * width, width), width)
+
+    def send(src, dst, ss, rs, where):
+        return pltpu.make_async_remote_copy(
+            src_ref=src,
+            dst_ref=dst,
+            send_sem=ss,
+            recv_sem=rs,
+            device_id=where,
+            device_id_type=pl.DeviceIdType.MESH,
+        )
+
+    def hid_copy(i):
+        rows = pl.ds(i * CHUNK, CHUNK)
+        return pltpu.make_async_copy(hidden_ref.at[:, rows], hid.at[:, rows], hid_sem.at[i])
+
+    for i in range(n_chunk):
+        hid_copy(i).start()
+
+    barrier = pltpu.get_barrier_semaphore()
+    for k in range(1, N_DP):
+        pl.semaphore_signal(
+            barrier, inc=1, device_id={"dp": zto(k)}, device_id_type=pl.DeviceIdType.MESH
+        )
+    for k in range(1, N_TP):
+        pl.semaphore_signal(
+            barrier,
+            inc=1,
+            device_id={"tensor": (t + k) % N_TP},
+            device_id_type=pl.DeviceIdType.MESH,
+        )
+    pl.semaphore_wait(barrier, N_DP + N_TP - 2)
+
+    def g_block(zi, ti):
+        return gbuf.at[zi, :, lanes(ti, share)]
+
+    def gz(k):
+        return send(
+            grads_ref, g_block(z, t), gz_ss.at[k - 1], gz_rs.at[k - 1], {"dp": zto(k)}
+        )
+
+    def gx(k):
+        block = g_block(zfrom(k), t)
+        return send(block, block, gx_ss.at[k], gx_rs.at[k], {"tensor": t_x})
+
+    def gc(k):
+        block = g_block(zfrom(k), t)
+        return send(block, block, gc_ss.at[k], gc_rs.at[k], {"tensor": t_c})
+
+    def gxc(k):
+        block = g_block(zfrom(k), t_x)
+        return send(block, block, gc_ss.at[4 + k], gc_rs.at[4 + k], {"tensor": t_c})
+
+    def gz_arrived(k):
+        block = g_block(zfrom(k), t)
+        return send(block, block, gz_ss.at[k - 1], gz_rs.at[k - 1], {"dp": zto(k)})
+
+    def gx_arrived(k):
+        block = g_block(zfrom(k), t_x)
+        return send(block, block, gx_ss.at[k], gx_rs.at[k], {"tensor": t_x})
+
+    def gc_arrived(k, ti):
+        block = g_block(zfrom(k % 4), ti)
+        return send(block, block, gc_ss.at[k], gc_rs.at[k], {"tensor": t_c})
+
+    gbuf[z, :, lanes(t, share)] = grads_ref[...]
+    for k in range(1, N_DP):
+        gz(k).start()
+    gx(0).start()
+    gc(0).start()
+
+    lane = lax.broadcasted_iota(jnp.int32, (32, 128), 1)
+    for i in range(n_chunk):
+        hid_copy(i).wait()
+
+        @pl.loop(0, CHUNK // 32)
+        def _(r, i=i):
+            rows = pl.ds(pl.multiple_of(i * CHUNK + r * 32, 32), 32)
+            sums = []
+            for layer in range(3):
+                values = hid[layer, rows, :].astype(F32)
+                sums.append(jnp.sum(values * values, axis=-1, keepdims=True))
+            sqcol[rows, :] = jnp.where(
+                lane == 0, sums[0], jnp.where(lane == 1, sums[1], sums[2])
+            )
+
+    sqsend[...] = sqcol[...].T[:8]
+
+    def sq(k):
+        return send(
+            sqsend,
+            sqrecv.at[k - 1],
+            sq_ss.at[k - 1],
+            sq_rs.at[k - 1],
+            {"tensor": (t + k) % N_TP},
+        )
+
+    for k in range(1, N_TP):
+        sq(k).start()
+    for k in range(1, N_TP):
+        sq(k).wait_recv()
+    total = sqsend[...] + sqrecv[0] + sqrecv[1] + sqrecv[2]
+    inverse = lax.rsqrt(total / D + epsilon) * live_ref[...]
+    invcol[...] = jnp.concatenate([inverse, jnp.zeros((120, tokens), F32)], axis=0).T
+
+    def jsend(k, i):
+        rows = pl.ds(i * CHUNK, CHUNK)
+        return send(
+            jloc.at[k - 1, rows],
+            jfeat.at[pl.ds(pl.multiple_of(z * tokens + i * CHUNK, CHUNK), CHUNK)],
+            j_ss.at[k - 1, i],
+            j_rs.at[k - 1, i],
+            {"dp": zto(k)},
+        )
+
+    def jarrived(k, i):
+        rows = pl.ds(pl.multiple_of(zfrom(k) * tokens + i * CHUNK, CHUNK), CHUNK)
+        return send(
+            jfeat.at[rows], jfeat.at[rows], j_ss.at[k - 1, i], j_rs.at[k - 1, i], {"dp": zto(k)}
+        )
+
+    for i in range(n_chunk):
+        for k in (1, 2, 3, 0):
+            cols = lanes(zto(k), feats)
+
+            @pl.loop(0, CHUNK // 16)
+            def _(r, i=i, k=k, cols=cols):
+                rows = pl.ds(pl.multiple_of(i * CHUNK + r * 16, 16), 16)
+                factors = invcol[rows, :]
+                mixture = jnp.zeros((16, feats), F32)
+                for layer in range(3):
+                    scaled = hid[layer, rows, cols].astype(F32) * gain_ref[pl.ds(layer, 1), cols]
+                    mixture = mixture + scaled * factors[:, layer : layer + 1]
+                if k:
+                    jloc[k - 1, rows, :] = mixture.astype(BF16)
+                else:
+                    mine = pl.ds(pl.multiple_of(z * tokens + i * CHUNK + r * 16, 16), 16)
+                    jfeat[mine, :] = mixture.astype(BF16)
+
+            if k:
+                jsend(k, i).start()
+
+    def kc(k):
+        return send(psend.at[k], precv.at[k], kc_ss.at[k], kc_rs.at[k], {"tensor": t_c})
+
+    def kx(k):
+        return send(xsend.at[k], xrecv.at[k], kx_ss.at[k], kx_rs.at[k], {"tensor": t_x})
+
+    def project(k):
+        if k:
+            for i in range(n_chunk):
+                jarrived(k, i).wait_recv()
+
+        @pl.loop(0, n_chunk)
+        def _(r):
+            rows = pl.ds(pl.multiple_of(r * CHUNK, CHUNK), CHUNK)
+            source = pl.ds(pl.multiple_of(zfrom(k) * tokens + r * CHUNK, CHUNK), CHUNK)
+            block = jfeat[source, :]
+            for half in range(2):
+                other = weight_ref[:, lanes(2 * half + 1 - c, share)]
+                psend[k, half, rows, :] = jnp.dot(
+                    block, other, preferred_element_type=F32
+                ).astype(BF16)
+            for half in range(2):
+                own = weight_ref[:, lanes(2 * half + c, share)]
+                pown[k, half, rows, :] = jnp.dot(block, own, preferred_element_type=F32)
+
+        kc(k).start()
+
+    def along_x(k):
+        kc(k).wait_recv()
+        base = zfrom(k) * tokens
+
+        @pl.loop(0, n_chunk)
+        def _(r):
+            rows = pl.ds(pl.multiple_of(r * CHUNK, CHUNK), CHUNK)
+            mine = pl.ds(pl.multiple_of(base + r * CHUNK, CHUNK), CHUNK)
+            xsend[k, rows, :] = (
+                pown[k, 1 - x, rows, :] + precv[k, 1 - x, rows, :].astype(F32)
+            ).astype(BF16)
+            keys[mine, :] = pown[k, x, rows, :] + precv[k, x, rows, :].astype(F32)
+
+        kx(k).start()
+
+    def along_x_done(k):
+        kx(k).wait_recv()
+        base = zfrom(k) * tokens
+
+        @pl.loop(0, n_chunk)
+        def _(r):
+            rows = pl.ds(pl.multiple_of(r * CHUNK, CHUNK), CHUNK)
+            mine = pl.ds(pl.multiple_of(base + r * CHUNK, CHUNK), CHUNK)
+            keysb[mine, :] = (keys[mine, :] + xrecv[k, rows, :].astype(F32)).astype(BF16)
+
+    def relay(k):
+        gz_arrived(k).wait_recv()
+        gx(k).start()
+        gc(k).start()
+
+    project(0)
+
+    row_ids = lax.broadcasted_iota(jnp.int32, (32, N_DP * tokens), 0)
+
+    @pl.loop(0, N_DP * tokens // 32)
+    def _(r):
+        rows = pl.ds(pl.multiple_of(r * 32, 32), 32)
+        order[rows, :] = jnp.where(dest_ref[...] == row_ids + r * 32, 1.0, 0.0).astype(BF16)
+
+    along_x(0)
+    for k in range(1, N_DP):
+        relay(k)
+        project(k)
+        along_x(k)
+        along_x_done(k - 1)
+        gx_arrived(k - 1).wait_recv()
+        gxc(k - 1).start()
+    along_x_done(N_DP - 1)
+
+    def kz(k):
+        return send(ksend.at[k], krecv.at[k - 1], kz_ss.at[k - 1], kz_rs.at[k - 1], {"dp": zto(k)})
+
+    for k in (1, 2, 3, 0):
+        owner = pl.ds(pl.multiple_of(zto(k) * tokens, tokens), tokens)
+        ksend[k] = jnp.dot(order[owner, :], keysb[...], preferred_element_type=F32).astype(BF16)
+        if k:
+            kz(k).start()
+    gx_arrived(N_DP - 1).wait_recv()
+    gxc(N_DP - 1).start()
+
+    @pl.loop(0, 2 * N_DP)
+    def _(b):
+        rows = pl.ds(pl.multiple_of(b * (tokens // 2), tokens // 2), tokens // 2)
+        jown[rows, :] = jnp.dot(
+            order[rows, :], jfeat[...], preferred_element_type=F32
+        ).astype(BF16)
+
+    @pl.loop(0, N_DP * n_chunk)
+    def _(b):
+        block = pl.ds(pl.multiple_of(b * CHUNK, CHUNK), CHUNK)
+        jturn[:, block] = jown[block, :].T
+
+    for k in range(N_DP):
+        gc_arrived(k, t_c).wait_recv()
+        gc_arrived(4 + k, t_xc).wait_recv()
+    for n in range(N_TP):
+        cols = pl.ds(n * share, share)
+
+        @pl.loop(0, feats // CHUNK)
+        def _(r, cols=cols):
+            rows = pl.ds(pl.multiple_of(r * CHUNK, CHUNK), CHUNK)
+            value = jnp.zeros((CHUNK, share), F32)
+            for d in range(N_DP):
+                value = value + jnp.dot(
+                    jturn[rows, pl.ds(d * tokens, tokens)],
+                    gbuf[d, :, cols],
+                    preferred_element_type=F32,
+                )
+            wgrad_ref[rows, cols] = value
+
+    for k in range(1, N_DP):
+        kz(k).wait_recv()
+    decay = decay_ref[...]
+    at_start = lax.broadcasted_iota(jnp.int32, (CHUNK, share), 0) % SEG == 0
+
+    def down(values):
+        return jnp.where(at_start, 0.0, pltpu.roll(values, 1, 0))
+
+    @pl.loop(0, n_chunk)
+    def _(r):
+        rows = pl.ds(pl.multiple_of(r * CHUNK, CHUNK), CHUNK)
+        value = ksend[0, rows, :].astype(F32)
+        for k in range(1, N_DP):
+            value = value + krecv[k - 1, rows, :].astype(F32)
+        second = value + decay * down(value)
+        third = value + decay * down(second)
+        states_ref[0, rows, :] = value.astype(BF16)
+        states_ref[1, rows, :] = second.astype(BF16)
+        states_ref[2, rows, :] = third.astype(BF16)
+
+    for k in range(1, N_DP):
+        gz(k).wait_send()
+        sq(k).wait_send()
+        kz(k).wait_send()
+        for i in range(n_chunk):
+            jsend(k, i).wait_send()
+    for k in range(N_DP):
+        gx(k).wait_send()
+        gc(k).wait_send()
+        gxc(k).wait_send()
+        kc(k).wait_send()
+        kx(k).wait_send()
+
+
+def fused(
+    hidden_rows,
+    layer_gain,
+    key_weight,
+    step_decay,
+    owner_list,
+    segment_len,
+    reweight_count,
+    loss_mask,
+    state_cotangent,
+):
+    dp_index = lax.axis_index("dp")
+    seg_count = N_DP * SEG_DEV
+    share = state_cotangent.shape[3]
+    tokens, layers, width = hidden_rows.shape
+    feats, key_width = key_weight.shape
+    ids = jnp.arange(seg_count)
+    same = owner_list[None, :] == owner_list[:, None]
+    rank = jnp.sum(same & (ids[None, :] < ids[:, None]), axis=1)
+    destination = owner_list * SEG_DEV + rank
+    source_of = jnp.sum(jnp.where(destination[None, :] == ids[:, None], ids[None, :], 0), axis=1)
+    my_source = lax.dynamic_slice_in_dim(source_of, dp_index * SEG_DEV, SEG_DEV, 0)
+
+    mask_table = loss_mask.reshape(seg_count, SEG).astype(F32)
+    scale_table = mask_table * reweight_count.astype(F32)[:, None]
+    pick = (my_source[:, None] == ids[None, :]).astype(F32)
+    scale_owner = jnp.sum(pick[:, :, None] * scale_table[None], axis=1)
+    state_grads = state_cotangent.astype(F32) * scale_owner[None, :, :, None]
+    key_grads = unrolled_grads(state_grads, step_decay).astype(BF16)
+    key_grads = key_grads.reshape(tokens, share)
+    my_len = lax.dynamic_slice_in_dim(segment_len, dp_index * SEG_DEV, SEG_DEV, 0)
+    live = (jnp.arange(SEG)[None, :] < my_len[:, None]).astype(F32).reshape(1, tokens)
+
+    dest_rows = (destination[:, None] * SEG + jnp.arange(SEG)[None, :]).reshape(1, -1)
+
+    vmem = pl.BlockSpec(memory_space=pltpu.VMEM)
+    dma = pltpu.SemaphoreType.DMA
+    n_chunk = tokens // CHUNK
+    states, weight_grad = pl.pallas_call(
+        fused_kernel,
+        out_shape=(
+            jax.ShapeDtypeStruct((3, tokens, share), BF16),
+            jax.ShapeDtypeStruct((feats, key_width), F32),
+        ),
+        in_specs=[
+            vmem,
+            pl.BlockSpec(memory_space=pl.ANY),
+            vmem,
+            vmem,
+            vmem,
+            vmem,
+            vmem,
+        ],
+        out_specs=(vmem, vmem),
+        scratch_shapes=[
+            pltpu.VMEM((layers, tokens, width), BF16),
+            pltpu.VMEM((tokens, 128), F32),
+            pltpu.VMEM((8, tokens), F32),
+            pltpu.VMEM((3, 8, tokens), F32),
+            pltpu.VMEM((tokens, 128), F32),
+            pltpu.VMEM((3, tokens, feats), BF16),
+            pltpu.VMEM((N_DP * tokens, feats), BF16),
+            pltpu.VMEM((N_DP * tokens, feats), BF16),
+            pltpu.VMEM((feats, N_DP * tokens), BF16),
+            pltpu.VMEM((N_DP * tokens, N_DP * tokens), BF16),
+            pltpu.VMEM((N_DP, tokens, key_width), BF16),
+            pltpu.VMEM((N_DP, 2, tokens, share), BF16),
+            pltpu.VMEM((N_DP, 2, tokens, share), BF16),
+            pltpu.VMEM((N_DP, 2, tokens, share), F32),
+            pltpu.VMEM((N_DP, tokens, share), BF16),
+            pltpu.VMEM((N_DP, tokens, share), BF16),
+            pltpu.VMEM((N_DP * tokens, share), F32),
+            pltpu.VMEM((N_DP * tokens, share), BF16),
+            pltpu.VMEM((N_DP, tokens, share), BF16),
+            pltpu.VMEM((N_DP - 1, tokens, share), BF16),
+            dma((n_chunk,)),
+            dma((3,)),
+            dma((3,)),
+            dma((3, n_chunk)),
+            dma((3, n_chunk)),
+            dma((3,)),
+            dma((3,)),
+            dma((4,)),
+            dma((4,)),
+            dma((8,)),
+            dma((8,)),
+            dma((4,)),
+            dma((4,)),
+            dma((4,)),
+            dma((4,)),
+            dma((3,)),
+            dma((3,)),
+        ],
+        compiler_params=pltpu.CompilerParams(
+            collective_id=0, has_side_effects=True, vmem_limit_bytes=56 * 1024 * 1024
+        ),
+        cost_estimate=pl.CostEstimate(
+            flops=4 * N_DP * tokens * feats * key_width,
+            bytes_accessed=12 * 1024 * 1024,
+            transcendentals=0,
+        ),
+        name="draft_head",
+    )(
+        dest_rows.astype(jnp.int32),
+        hidden_rows.transpose(1, 0, 2),
+        layer_gain,
+        live,
+        key_weight,
+        step_decay.reshape(1, share),
+        key_grads,
+    )
+    return (states.reshape(3, SEG_DEV, SEG, share), weight_grad)
+
+
+def uses_kernel(mesh):
+    return mesh.shape["dp"] == N_DP and mesh.shape["tensor"] == N_TP
+
+
 def solution(mesh):
     return jax.shard_map(
-        per_device,
+        fused if uses_kernel(mesh) else per_device,
         mesh=mesh,
         in_specs=(
             P(("groups", "dp"), None, "tensor"),

time: 644 us -> 139 us (0.22)
  waiting for transfers between devices: 547 us -> 0 us
  Pallas kernels: 0 us -> 124 us
  other arithmetic: 25.1 us -> 5.88 us
  local copies, waits for them, and re-layouts: 23.3 us -> 8.21 us
  matrix products: 14.1 us -> 0 us
  between operations: 14 us -> 0.74 us
  blocking collectives: 11.1 us -> 0 us
  starting transfers between devices: 6.83 us -> 0 us
    all_to_all x1 -> x0, waiting for transfers between devices: 334 us -> none  [per_device(): lax.all_to_all(outgoing, 'dp', split_axis=0, concat_axis=0, tiled=True)]
    reduce_scatter x1 -> x0, waiting for transfers between devices: 143 us -> none  [per_device(): lax.psum_scatter(lax.dot_general(columns, flat_grads, (((0,), (0,)), ((),...]
    pallas_call x0 -> x1, Pallas kernels: none -> 124 us  [fused(): pl.pallas_call(fused_kernel, out_shape=(jax.ShapeDtypeStruct((3, tokens,...]
    psum x1 -> x0, waiting for transfers between devices: 51.5 us -> none  [per_device(): summed_keys = lax.psum(partial_keys, 'tensor')]
    gather x5 -> x0, local copies, waits for them, and re-layouts: 19.9 us -> none  [the longest x1 9.82 us: per_device(): row_block[send_pick]]
    all_gather x2 -> x0, waiting for transfers between devices: 17.4 us -> none  [the longest x1 17.3 us: per_device(): all_grads = lax.all_gather(key_grads, 'tensor', axis=2, tiled=True)]
    dot_general x2 -> x0, matrix products: 14.1 us -> none  [the longest x1 8.18 us: per_device(): lax.dot_general(columns, flat_grads, (((0,), (0,)), ((), ())), preferred_...]
    psum x1 -> x0, blocking collectives: 11.1 us -> none  [per_device(): squares = lax.psum(layer_squares(owner_rows), 'tensor')]
  transfers between devices with their start and end apart: 5 -> 0, of which waited for: 4 -> 0; matrix products, arithmetic and copies ran while one was open for 3% -> 0% of each run, Pallas kernels for 0% -> 0%
where the time goes in v1:
time: 139 us
  Pallas kernels  124 us (89%)
  local copies, waits for them, and re-layouts  8.21 us (6%)
  other arithmetic  5.88 us (4%)
    pallas_call x1, Pallas kernels, fused(): pl.pallas_call(fused_kernel, out_shape=(jax.ShapeDtypeStruct((3, tokens,...  124 us
    unnamed x4, local copies, waits for them, and re-layouts  5.8 us

profile of v1, /device:TPU:9, one launch (start us, length us, event | category | flops | bytes accessed | tf_op | source)
XLA Modules:
  0.0 138.7 jit_solution(1087163676509497399)
XLA Ops:
  0.6 0.7 dynamic_slice.6
  1.4 0.7 convert_element_type.49
  2.0 0.9 convert_reduce_fusion
  2.9 0.7 broadcast_multiply_fusion.1
  3.6 0.1 select_reduce_fusion
  3.7 0.1 dynamic_slice.7
  3.8 0.7 convert_element_type.47
  4.5 0.1 fusion.7
  4.6 0.1 fusion.6
  4.6 0.7 reshape.116.live_ref
  5.3 0.1 convert_element_type.48
  5.4 0.1 broadcast_multiply_fusion
  5.5 0.1 copy.11
  5.5 0.2 multiply_reduce_fusion
  5.7 0.1 iota_add_fusion
  5.8 0.7 add.50.dest_ref
  6.5 1.4 convert_multiply_fusion
  7.8 0.0 copy-start
  7.9 0.6 copy-done
  8.5 0.1 fusion
  8.7 0.9 fusion.4
  9.6 123.9 %draft_head.1 = (bf16[3,512,256]{2,1,0:T(8,128)(2,1)}, f32[512,1024]{1,0:T(8,128)}) custom-call(s32[1,2048]{1,0:T(1,128)} %add.50.dest_ref, bf16[3,512,2048]{2,1,0:T(8,128)(2,1)} %bitcast.25, f32[3,2048]{1,0:T(4,128)} %gain_ref.1, f32[1,512]{1,0:T(1,128)} %reshape.116.live_ref, bf16[512,1024]{1,0:T(8,128)(2,1)} %weight_ref.1, f32[1,256]{1,0:T(1,128)} %bitcast.24, ...), custom_call_target="tpu_custom_call" | custom-call | flops 4294967296 | bytes 12582912 | tf_op jit(solution)/shard_map/draft_head/pallas_call | solution.py:534
  133.5 2.1 %copy.14 = bf16[3,32,16,256]{3,2,1,0:T(8,128)(2,1)} copy(bf16[3,32,16,256]{3,2,1,0:T(8,128)(2,1)} %bitcast.22) | data formatting | bytes 1572864
  135.6 3.2 %copy.15 = f32[512,1024]{1,0:T(8,128)} copy(f32[512,1024]{1,0:T(8,128)} %get-tuple-element.11) | data formatting | bytes 4194304
  (3 shorter events, 0.1 us)
Async XLA Ops:
  7.8 0.7 copy-start

commit v2 on v1

--- a/solution.py
+++ b/solution.py
@@ -134,16 +134,20 @@
 
 
 def fused_kernel(
-    dest_ref,
+    owner_ref,
+    length_ref,
+    count_ref,
+    mask_ref,
     hidden_ref,
     gain_ref,
-    live_ref,
     weight_ref,
     decay_ref,
-    grads_ref,
+    cotangent_ref,
     states_ref,
     wgrad_ref,
     hid,
+    dest,
+    grads,
     sqcol,
     sqsend,
     sqrecv,
@@ -161,6 +165,7 @@
     xrecv,
     keys,
     keysb,
+    kpart,
     ksend,
     krecv,
     hid_sem,
@@ -190,7 +195,7 @@
     t_xc = (t_c + 2) % N_TP
     tokens = hid.shape[1]
     feats = weight_ref.shape[0]
-    share = grads_ref.shape[1]
+    share = grads.shape[1]
     n_chunk = tokens // CHUNK
 
     def zto(k):
@@ -233,43 +238,146 @@
         )
     pl.semaphore_wait(barrier, N_DP + N_TP - 2)
 
+    seg_count = N_DP * SEG_DEV
+    all_tokens = N_DP * tokens
+    square = (seg_count, seg_count)
+    owner_row = owner_ref[...].astype(F32)
+    across = jnp.broadcast_to(owner_row, square)
+    earlier = lax.broadcasted_iota(jnp.int32, square, 0) < lax.broadcasted_iota(
+        jnp.int32, square, 1
+    )
+    match = jnp.where(earlier, jnp.where(across == across.T, 1.0, 0.0), 0.0)
+    dest_seg = owner_row * SEG_DEV + jnp.sum(match, axis=0, keepdims=True)
+    sub = lax.broadcasted_iota(jnp.int32, (8, seg_count), 0)
+    rows8 = jnp.where(
+        sub == 0,
+        dest_seg,
+        jnp.where(sub == 1, count_ref[...].astype(F32), length_ref[...].astype(F32)),
+    ).astype(BF16)
+
+    def spread(first, width):
+        shape = (seg_count, width)
+        token_seg = lax.broadcasted_iota(jnp.int32, shape, 1) // SEG + first
+        hot = jnp.where(lax.broadcasted_iota(jnp.int32, shape, 0) == token_seg, 1.0, 0.0)
+        return jnp.dot(rows8, hot.astype(BF16), preferred_element_type=F32)
+
+    whole = spread(0, all_tokens)
+    place = (lax.broadcasted_iota(jnp.int32, (1, all_tokens), 1) % SEG).astype(F32)
+    dest[...] = whole[0:1] * SEG + place
+    scale_row = whole[1:2] * mask_ref[...].astype(F32)
+    scale_rows = jnp.broadcast_to(scale_row, (128, all_tokens)).astype(BF16)
+    here = spread(z * SEG_DEV, tokens)
+    live = jnp.where(place[:, :tokens] < here[2:3], 1.0, 0.0)
+
+    def fill_order(first, count):
+        @pl.loop(0, count // 16)
+        def _(r):
+            start = pl.multiple_of(first + r * 16, 16)
+            ids = lax.broadcasted_iota(jnp.int32, (16, all_tokens), 0) + start
+            order[pl.ds(start, 16), :] = jnp.where(dest[...] == ids.astype(F32), 1.0, 0.0).astype(
+                BF16
+            )
+
+    fill_order(z * tokens, tokens)
+
+    decay = decay_ref[...]
+    positions = lax.broadcasted_iota(jnp.int32, (CHUNK, share), 0) % SEG
+
+    def down(values):
+        return jnp.where(positions == 0, 0.0, pltpu.roll(values, 1, 0))
+
+    def up(values):
+        return jnp.where(positions == SEG - 1, 0.0, pltpu.roll(values, CHUNK - 1, 0))
+
+    for r in range(n_chunk):
+        rows = pl.ds(r * CHUNK, CHUNK)
+        mine = pl.ds(pl.multiple_of(z * tokens + r * CHUNK, CHUNK), CHUNK)
+        scale = lax.dot_general(
+            order[mine, :], scale_rows, (((1,), (1,)), ((), ())), preferred_element_type=F32
+        )
+        scale = jnp.concatenate([scale] * (share // 128), axis=1)
+        third = cotangent_ref[2, rows, :].astype(F32) * scale
+        second = cotangent_ref[1, rows, :].astype(F32) * scale + decay * up(third)
+        first = cotangent_ref[0, rows, :].astype(F32) * scale + decay * up(second)
+        total = (first + second + third).astype(BF16)
+        grads[rows, :] = total
+        gbuf[z, rows, lanes(t, share)] = total
+
     def g_block(zi, ti):
         return gbuf.at[zi, :, lanes(ti, share)]
 
-    def gz(k):
+    def gz(side, hop):
+        step = 1 - 2 * side
+        src = z - step * hop
+        block = g_block(src, t)
         return send(
-            grads_ref, g_block(z, t), gz_ss.at[k - 1], gz_rs.at[k - 1], {"dp": zto(k)}
-        )
-
-    def gx(k):
-        block = g_block(zfrom(k), t)
-        return send(block, block, gx_ss.at[k], gx_rs.at[k], {"tensor": t_x})
-
-    def gc(k):
-        block = g_block(zfrom(k), t)
+            grads if hop == 0 else block,
+            block,
+            gz_ss.at[side, hop],
+            gz_rs.at[side, hop],
+            {"dp": z + step},
+        )
+
+    def gx(d):
+        block = g_block(d, t)
+        return send(block, block, gx_ss.at[d], gx_rs.at[d], {"tensor": t_x})
+
+    def gc(d):
+        block = g_block(d, t)
+        return send(block, block, gc_ss.at[d], gc_rs.at[d], {"tensor": t_c})
+
+    def gxc(d):
+        block = g_block(d, t_x)
+        return send(block, block, gc_ss.at[4 + d], gc_rs.at[4 + d], {"tensor": t_c})
+
+    def gz_arrived(side, hop):
+        step = 1 - 2 * side
+        block = g_block(z - step * hop, t)
+        return send(
+            block, block, gz_ss.at[side, hop - 1], gz_rs.at[side, hop - 1], {"dp": z - step}
+        )
+
+    def gx_arrived(d):
+        block = g_block(d, t_x)
+        return send(block, block, gx_ss.at[d], gx_rs.at[d], {"tensor": t_x})
+
+    def gc_arrived(k, ti):
+        block = g_block(k % 4, ti)
         return send(block, block, gc_ss.at[k], gc_rs.at[k], {"tensor": t_c})
 
-    def gxc(k):
-        block = g_block(zfrom(k), t_x)
-        return send(block, block, gc_ss.at[4 + k], gc_rs.at[4 + k], {"tensor": t_c})
-
-    def gz_arrived(k):
-        block = g_block(zfrom(k), t)
-        return send(block, block, gz_ss.at[k - 1], gz_rs.at[k - 1], {"dp": zto(k)})
-
-    def gx_arrived(k):
-        block = g_block(zfrom(k), t_x)
-        return send(block, block, gx_ss.at[k], gx_rs.at[k], {"tensor": t_x})
-
-    def gc_arrived(k, ti):
-        block = g_block(zfrom(k % 4), ti)
-        return send(block, block, gc_ss.at[k], gc_rs.at[k], {"tensor": t_c})
-
-    gbuf[z, :, lanes(t, share)] = grads_ref[...]
-    for k in range(1, N_DP):
-        gz(k).start()
-    gx(0).start()
-    gc(0).start()
+    def came(side, hop):
+        return z >= hop if side == 0 else z + hop < N_DP
+
+    def goes(side, hop):
+        return came(side, hop) & (z < N_DP - 1 if side == 0 else z > 0)
+
+    def pass_on(hop):
+        for side in range(2):
+
+            @pl.when(goes(side, hop))
+            def _(side=side):
+                gz(side, hop).start()
+
+    pass_on(0)
+    gx(z).start()
+    gc(z).start()
+
+    def relay(hop):
+        for side in range(2):
+
+            @pl.when(came(side, hop))
+            def _(side=side):
+                gz_arrived(side, hop).wait_recv()
+
+        if hop < N_DP - 1:
+            pass_on(hop)
+        for side in range(2):
+
+            @pl.when(came(side, hop))
+            def _(side=side):
+                src = z - (1 - 2 * side) * hop
+                gx(src).start()
+                gc(src).start()
 
     lane = lax.broadcasted_iota(jnp.int32, (32, 128), 1)
     for i in range(n_chunk):
@@ -302,7 +410,7 @@
     for k in range(1, N_TP):
         sq(k).wait_recv()
     total = sqsend[...] + sqrecv[0] + sqrecv[1] + sqrecv[2]
-    inverse = lax.rsqrt(total / D + epsilon) * live_ref[...]
+    inverse = lax.rsqrt(total / D + epsilon) * live
     invcol[...] = jnp.concatenate([inverse, jnp.zeros((120, tokens), F32)], axis=0).T
 
     def jsend(k, i):
@@ -341,93 +449,124 @@
 
             if k:
                 jsend(k, i).start()
-
-    def kc(k):
-        return send(psend.at[k], precv.at[k], kc_ss.at[k], kc_rs.at[k], {"tensor": t_c})
-
-    def kx(k):
-        return send(xsend.at[k], xrecv.at[k], kx_ss.at[k], kx_rs.at[k], {"tensor": t_x})
-
-    def project(k):
-        if k:
-            for i in range(n_chunk):
-                jarrived(k, i).wait_recv()
-
-        @pl.loop(0, n_chunk)
-        def _(r):
-            rows = pl.ds(pl.multiple_of(r * CHUNK, CHUNK), CHUNK)
-            source = pl.ds(pl.multiple_of(zfrom(k) * tokens + r * CHUNK, CHUNK), CHUNK)
-            block = jfeat[source, :]
-            for half in range(2):
-                other = weight_ref[:, lanes(2 * half + 1 - c, share)]
-                psend[k, half, rows, :] = jnp.dot(
-                    block, other, preferred_element_type=F32
-                ).astype(BF16)
-            for half in range(2):
-                own = weight_ref[:, lanes(2 * half + c, share)]
-                pown[k, half, rows, :] = jnp.dot(block, own, preferred_element_type=F32)
-
-        kc(k).start()
-
-    def along_x(k):
-        kc(k).wait_recv()
-        base = zfrom(k) * tokens
-
-        @pl.loop(0, n_chunk)
-        def _(r):
-            rows = pl.ds(pl.multiple_of(r * CHUNK, CHUNK), CHUNK)
-            mine = pl.ds(pl.multiple_of(base + r * CHUNK, CHUNK), CHUNK)
-            xsend[k, rows, :] = (
-                pown[k, 1 - x, rows, :] + precv[k, 1 - x, rows, :].astype(F32)
-            ).astype(BF16)
-            keys[mine, :] = pown[k, x, rows, :] + precv[k, x, rows, :].astype(F32)
-
-        kx(k).start()
-
-    def along_x_done(k):
-        kx(k).wait_recv()
-        base = zfrom(k) * tokens
-
-        @pl.loop(0, n_chunk)
-        def _(r):
-            rows = pl.ds(pl.multiple_of(r * CHUNK, CHUNK), CHUNK)
-            mine = pl.ds(pl.multiple_of(base + r * CHUNK, CHUNK), CHUNK)
-            keysb[mine, :] = (keys[mine, :] + xrecv[k, rows, :].astype(F32)).astype(BF16)
-
-    def relay(k):
-        gz_arrived(k).wait_recv()
-        gx(k).start()
-        gc(k).start()
-
-    project(0)
-
-    row_ids = lax.broadcasted_iota(jnp.int32, (32, N_DP * tokens), 0)
-
-    @pl.loop(0, N_DP * tokens // 32)
-    def _(r):
-        rows = pl.ds(pl.multiple_of(r * 32, 32), 32)
-        order[rows, :] = jnp.where(dest_ref[...] == row_ids + r * 32, 1.0, 0.0).astype(BF16)
-
-    along_x(0)
+        if i:
+            relay(i)
+
+    n_unit = N_DP * n_chunk
+
+    def unit_rows(u):
+        far = jnp.where(u < n_chunk, 0, (u + 3 * N_DP - n_chunk) % (N_DP - 1) + 1)
+        part = jnp.where(u < n_chunk, u, (u + 3 * N_DP - n_chunk) // (N_DP - 1) - N_DP)
+        return far, part, pl.multiple_of(zfrom(far) * tokens + part * CHUNK, CHUNK)
+
+    def kc(u):
+        return send(psend.at[u], precv.at[u], kc_ss.at[u], kc_rs.at[u], {"tensor": t_c})
+
+    def kx(u):
+        return send(xsend.at[u], xrecv.at[u], kx_ss.at[u], kx_rs.at[u], {"tensor": t_x})
+
+    def project(u):
+        _, _, start = unit_rows(u)
+        block = jfeat[pl.ds(start, CHUNK), :]
+        for half in range(2):
+            other = weight_ref[:, lanes(2 * half + 1 - c, share)]
+            psend[u, half] = jnp.dot(block, other, preferred_element_type=F32).astype(BF16)
+        kc(u).start()
+        for half in range(2):
+            own = weight_ref[:, lanes(2 * half + c, share)]
+            pown[u, half] = jnp.dot(block, own, preferred_element_type=F32)
+
+    def along_x(u):
+        kc(u).wait_recv()
+        _, _, start = unit_rows(u)
+        xsend[u] = (pown[u, 1 - x] + precv[u, 1 - x].astype(F32)).astype(BF16)
+        kx(u).start()
+        keys[pl.ds(start, CHUNK), :] = pown[u, x] + precv[u, x].astype(F32)
+
+    def along_x_done(u):
+        kx(u).wait_recv()
+        _, _, start = unit_rows(u)
+        mine = pl.ds(start, CHUNK)
+        keysb[mine, :] = (keys[mine, :] + xrecv[u].astype(F32)).astype(BF16)
+
     for k in range(1, N_DP):
-        relay(k)
-        project(k)
-        along_x(k)
-        along_x_done(k - 1)
-        gx_arrived(k - 1).wait_recv()
-        gxc(k - 1).start()
-    along_x_done(N_DP - 1)
-
-    def kz(k):
-        return send(ksend.at[k], krecv.at[k - 1], kz_ss.at[k - 1], kz_rs.at[k - 1], {"dp": zto(k)})
-
-    for k in (1, 2, 3, 0):
-        owner = pl.ds(pl.multiple_of(zto(k) * tokens, tokens), tokens)
-        ksend[k] = jnp.dot(order[owner, :], keysb[...], preferred_element_type=F32).astype(BF16)
-        if k:
-            kz(k).start()
-    gx_arrived(N_DP - 1).wait_recv()
-    gxc(N_DP - 1).start()
+        fill_order(zto(k) * tokens, tokens)
+
+    @pl.loop(0, n_unit + 2)
+    def _(step):
+        @pl.when((step >= n_chunk) & (step < n_unit))
+        def _():
+            far, part, _ = unit_rows(step)
+            jarrived(far, part).wait_recv()
+
+        @pl.when(step < n_unit)
+        def _():
+            project(step)
+
+        @pl.when((step >= 1) & (step <= n_unit))
+        def _():
+            along_x(step - 1)
+
+        @pl.when(step >= 2)
+        def _():
+            along_x_done(step - 2)
+
+    def kz(side, o):
+        return send(
+            ksend.at[o],
+            krecv.at[side, o],
+            kz_ss.at[side, o],
+            kz_rs.at[side, o],
+            {"dp": z + 1 - 2 * side},
+        )
+
+    def kz_arrived(side, o):
+        return send(
+            ksend.at[o],
+            krecv.at[side, o],
+            kz_ss.at[side, o],
+            kz_rs.at[side, o],
+            {"dp": z - 1 + 2 * side},
+        )
+
+    def own_part(o):
+        return jnp.dot(
+            order[o * tokens : (o + 1) * tokens, :], keysb[...], preferred_element_type=F32
+        )
+
+    last = N_DP - 1
+
+    @pl.when(z == 0)
+    def _():
+        for o in (3, 2, 1):
+            ksend[o] = own_part(o).astype(BF16)
+            kz(0, o).start()
+        kpart[0] = own_part(0)
+
+    @pl.when(z == last)
+    def _():
+        for o in (0, 1, 2):
+            ksend[o] = own_part(o).astype(BF16)
+            kz(1, o).start()
+        kpart[3] = own_part(3)
+
+    @pl.when((z > 0) & (z < last))
+    def _():
+        for o in range(N_DP):
+            kpart[o] = own_part(o)
+
+    def stage(j):
+        for side, o in ((0, last - j), (1, j)):
+
+            @pl.when((z > 0) & (z < last) & (z < o if side == 0 else z > o))
+            def _(side=side, o=o):
+                kz_arrived(side, o).wait_recv()
+                ksend[o] = (kpart[o] + krecv[side, o].astype(F32)).astype(BF16)
+                kz(side, o).start()
+
+    for d in range(N_DP):
+        gx_arrived(d).wait_recv()
+        gxc(d).start()
 
     @pl.loop(0, 2 * N_DP)
     def _(b):
@@ -441,10 +580,13 @@
         block = pl.ds(pl.multiple_of(b * CHUNK, CHUNK), CHUNK)
         jturn[:, block] = jown[block, :].T
 
+    stage(0)
     for k in range(N_DP):
         gc_arrived(k, t_c).wait_recv()
         gc_arrived(4 + k, t_xc).wait_recv()
     for n in range(N_TP):
+        if n == 2:
+            stage(1)
         cols = pl.ds(n * share, share)
 
         @pl.loop(0, feats // CHUNK)
@@ -459,20 +601,22 @@
                 )
             wgrad_ref[rows, cols] = value
 
-    for k in range(1, N_DP):
-        kz(k).wait_recv()
-    decay = decay_ref[...]
-    at_start = lax.broadcasted_iota(jnp.int32, (CHUNK, share), 0) % SEG == 0
-
-    def down(values):
-        return jnp.where(at_start, 0.0, pltpu.roll(values, 1, 0))
+    stage(2)
+
+    @pl.when(z > 0)
+    def _():
+        kz_arrived(0, z).wait_recv()
+        kpart[z] = kpart[z] + krecv[0, z].astype(F32)
+
+    @pl.when(z < last)
+    def _():
+        kz_arrived(1, z).wait_recv()
+        kpart[z] = kpart[z] + krecv[1, z].astype(F32)
 
     @pl.loop(0, n_chunk)
     def _(r):
         rows = pl.ds(pl.multiple_of(r * CHUNK, CHUNK), CHUNK)
-        value = ksend[0, rows, :].astype(F32)
-        for k in range(1, N_DP):
-            value = value + krecv[k - 1, rows, :].astype(F32)
+        value = kpart[z, rows, :]
         second = value + decay * down(value)
         third = value + decay * down(second)
         states_ref[0, rows, :] = value.astype(BF16)
@@ -480,17 +624,33 @@
         states_ref[2, rows, :] = third.astype(BF16)
 
     for k in range(1, N_DP):
-        gz(k).wait_send()
         sq(k).wait_send()
-        kz(k).wait_send()
         for i in range(n_chunk):
             jsend(k, i).wait_send()
-    for k in range(N_DP):
-        gx(k).wait_send()
-        gc(k).wait_send()
-        gxc(k).wait_send()
-        kc(k).wait_send()
-        kx(k).wait_send()
+    for hop in range(N_DP - 1):
+        for side in range(2):
+
+            @pl.when(goes(side, hop))
+            def _(side=side, hop=hop):
+                gz(side, hop).wait_send()
+
+    for d in range(N_DP):
+        gx(d).wait_send()
+        gc(d).wait_send()
+        gxc(d).wait_send()
+
+        @pl.when(z < d)
+        def _(d=d):
+            kz(0, d).wait_send()
+
+        @pl.when(z > d)
+        def _(d=d):
+            kz(1, d).wait_send()
+
+    @pl.loop(0, n_unit)
+    def _(u):
+        kc(u).wait_send()
+        kx(u).wait_send()
 
 
 def fused(
@@ -504,33 +664,14 @@
     loss_mask,
     state_cotangent,
 ):
-    dp_index = lax.axis_index("dp")
-    seg_count = N_DP * SEG_DEV
     share = state_cotangent.shape[3]
     tokens, layers, width = hidden_rows.shape
     feats, key_width = key_weight.shape
-    ids = jnp.arange(seg_count)
-    same = owner_list[None, :] == owner_list[:, None]
-    rank = jnp.sum(same & (ids[None, :] < ids[:, None]), axis=1)
-    destination = owner_list * SEG_DEV + rank
-    source_of = jnp.sum(jnp.where(destination[None, :] == ids[:, None], ids[None, :], 0), axis=1)
-    my_source = lax.dynamic_slice_in_dim(source_of, dp_index * SEG_DEV, SEG_DEV, 0)
-
-    mask_table = loss_mask.reshape(seg_count, SEG).astype(F32)
-    scale_table = mask_table * reweight_count.astype(F32)[:, None]
-    pick = (my_source[:, None] == ids[None, :]).astype(F32)
-    scale_owner = jnp.sum(pick[:, :, None] * scale_table[None], axis=1)
-    state_grads = state_cotangent.astype(F32) * scale_owner[None, :, :, None]
-    key_grads = unrolled_grads(state_grads, step_decay).astype(BF16)
-    key_grads = key_grads.reshape(tokens, share)
-    my_len = lax.dynamic_slice_in_dim(segment_len, dp_index * SEG_DEV, SEG_DEV, 0)
-    live = (jnp.arange(SEG)[None, :] < my_len[:, None]).astype(F32).reshape(1, tokens)
-
-    dest_rows = (destination[:, None] * SEG + jnp.arange(SEG)[None, :]).reshape(1, -1)
 
     vmem = pl.BlockSpec(memory_space=pltpu.VMEM)
     dma = pltpu.SemaphoreType.DMA
     n_chunk = tokens // CHUNK
+    n_unit = N_DP * n_chunk
     states, weight_grad = pl.pallas_call(
         fused_kernel,
         out_shape=(
@@ -539,8 +680,10 @@
         ),
         in_specs=[
             vmem,
+            vmem,
+            vmem,
+            vmem,
             pl.BlockSpec(memory_space=pl.ANY),
-            vmem,
             vmem,
             vmem,
             vmem,
@@ -549,6 +692,8 @@
         out_specs=(vmem, vmem),
         scratch_shapes=[
             pltpu.VMEM((layers, tokens, width), BF16),
+            pltpu.VMEM((1, N_DP * tokens), F32),
+            pltpu.VMEM((tokens, share), BF16),
             pltpu.VMEM((tokens, 128), F32),
             pltpu.VMEM((8, tokens), F32),
             pltpu.VMEM((3, 8, tokens), F32),
@@ -559,35 +704,36 @@
             pltpu.VMEM((feats, N_DP * tokens), BF16),
             pltpu.VMEM((N_DP * tokens, N_DP * tokens), BF16),
             pltpu.VMEM((N_DP, tokens, key_width), BF16),
-            pltpu.VMEM((N_DP, 2, tokens, share), BF16),
-            pltpu.VMEM((N_DP, 2, tokens, share), BF16),
-            pltpu.VMEM((N_DP, 2, tokens, share), F32),
-            pltpu.VMEM((N_DP, tokens, share), BF16),
-            pltpu.VMEM((N_DP, tokens, share), BF16),
+            pltpu.VMEM((n_unit, 2, CHUNK, share), BF16),
+            pltpu.VMEM((n_unit, 2, CHUNK, share), BF16),
+            pltpu.VMEM((n_unit, 2, CHUNK, share), F32),
+            pltpu.VMEM((n_unit, CHUNK, share), BF16),
+            pltpu.VMEM((n_unit, CHUNK, share), BF16),
             pltpu.VMEM((N_DP * tokens, share), F32),
             pltpu.VMEM((N_DP * tokens, share), BF16),
+            pltpu.VMEM((N_DP, tokens, share), F32),
             pltpu.VMEM((N_DP, tokens, share), BF16),
-            pltpu.VMEM((N_DP - 1, tokens, share), BF16),
+            pltpu.VMEM((2, N_DP, tokens, share), BF16),
             dma((n_chunk,)),
             dma((3,)),
             dma((3,)),
             dma((3, n_chunk)),
             dma((3, n_chunk)),
-            dma((3,)),
-            dma((3,)),
+            dma((2, 3)),
+            dma((2, 3)),
             dma((4,)),
             dma((4,)),
             dma((8,)),
             dma((8,)),
-            dma((4,)),
-            dma((4,)),
-            dma((4,)),
-            dma((4,)),
-            dma((3,)),
-            dma((3,)),
+            dma((n_unit,)),
+            dma((n_unit,)),
+            dma((n_unit,)),
+            dma((n_unit,)),
+            dma((2, 4)),
+            dma((2, 4)),
         ],
         compiler_params=pltpu.CompilerParams(
-            collective_id=0, has_side_effects=True, vmem_limit_bytes=56 * 1024 * 1024
+            collective_id=0, has_side_effects=True, vmem_limit_bytes=60 * 1024 * 1024
         ),
         cost_estimate=pl.CostEstimate(
             flops=4 * N_DP * tokens * feats * key_width,
@@ -596,13 +742,15 @@
         ),
         name="draft_head",
     )(
-        dest_rows.astype(jnp.int32),
+        owner_list.reshape(1, -1),
+        segment_len.reshape(1, -1),
+        reweight_count.reshape(1, -1),
+        loss_mask.reshape(1, -1),
         hidden_rows.transpose(1, 0, 2),
         layer_gain,
-        live,
         key_weight,
         step_decay.reshape(1, share),
-        key_grads,
+        state_cotangent.reshape(3, tokens, share),
     )
     return (states.reshape(3, SEG_DEV, SEG, share), weight_grad)
 

time: 139 us -> 148 us (1.065)
  the two profiles are of different devices: /device:TPU:9 before, /device:TPU:20 now
where the time goes in v2:
time: 148 us
  Pallas kernels  142 us (96%)
  local copies, waits for them, and re-layouts  5.22 us (4%)
    pallas_call x1, Pallas kernels, fused(): pl.pallas_call(fused_kernel, out_shape=(jax.ShapeDtypeStruct((3, tokens,...  142 us
    unnamed x2, local copies, waits for them, and re-layouts  5.22 us

profile of v2, /device:TPU:20, one launch (start us, length us, event | category | flops | bytes accessed | tf_op | source)
XLA Modules:
  0.0 147.9 jit_solution(16838017675717074747)
XLA Ops:
  0.6 142.0 %draft_head.1 = (bf16[3,512,256]{2,1,0:T(8,128)(2,1)}, f32[512,1024]{1,0:T(8,128)}) custom-call(s32[1,128]{1,0:T(1,128)} %bitcast.13, s32[1,128]{1,0:T(1,128)} %bitcast.14, s32[1,128]{1,0:T(1,128)} %bitcast.15, s32[1,2048]{1,0:T(1,128)} %bitcast.11, bf16[3,512,2048]{2,1,0:T(8,128)(2,1)} %bitcast.9, f32[3,2048]{1,0:T(4,128)} %gain_ref.1, ...), custom_call_target="tpu_custom_call" | custom-call | flops 4294967296 | bytes 12582912 | tf_op jit(solution)/shard_map/draft_head/pallas_call | solution.py:675
  142.6 2.1 %copy.13 = bf16[3,32,16,256]{3,2,1,0:T(8,128)(2,1)} copy(bf16[3,32,16,256]{3,2,1,0:T(8,128)(2,1)} %bitcast.8) | data formatting | bytes 1572864
  144.7 3.2 %copy.14 = f32[512,1024]{1,0:T(8,128)} copy(f32[512,1024]{1,0:T(8,128)} %get-tuple-element.9) | data formatting | bytes 4194304

commit v3 on v2

--- a/solution.py
+++ b/solution.py
@@ -238,6 +238,34 @@
         )
     pl.semaphore_wait(barrier, N_DP + N_TP - 2)
 
+    lane = lax.broadcasted_iota(jnp.int32, (32, 128), 1)
+    for i in range(n_chunk):
+        hid_copy(i).wait()
+
+        @pl.loop(0, CHUNK // 32)
+        def _(r, i=i):
+            rows = pl.ds(pl.multiple_of(i * CHUNK + r * 32, 32), 32)
+            sums = []
+            for layer in range(3):
+                values = hid[layer, rows, :].astype(F32)
+                sums.append(jnp.sum(values * values, axis=-1, keepdims=True))
+            sqcol[rows, :] = jnp.where(
+                lane == 0, sums[0], jnp.where(lane == 1, sums[1], sums[2])
+            )
+
+    sqsend[...] = sqcol[...].T[:8]
+
+    def sq(k):
+        return send(
+            sqsend,
+            sqrecv.at[k - 1],
+            sq_ss.at[k - 1],
+            sq_rs.at[k - 1],
+            {"tensor": (t + k) % N_TP},
+        )
+
+    for k in range(1, N_TP):
+        sq(k).start()
     seg_count = N_DP * SEG_DEV
     all_tokens = N_DP * tokens
     square = (seg_count, seg_count)
@@ -270,13 +298,17 @@
     live = jnp.where(place[:, :tokens] < here[2:3], 1.0, 0.0)
 
     def fill_order(first, count):
-        @pl.loop(0, count // 16)
+        @pl.loop(0, count // 32)
         def _(r):
-            start = pl.multiple_of(first + r * 16, 16)
-            ids = lax.broadcasted_iota(jnp.int32, (16, all_tokens), 0) + start
-            order[pl.ds(start, 16), :] = jnp.where(dest[...] == ids.astype(F32), 1.0, 0.0).astype(
-                BF16
-            )
+            for half in range(2):
+                start = pl.multiple_of(first + r * 32 + half * 16, 16)
+                ids = lax.broadcasted_iota(jnp.int32, (16, 128), 0) + start
+                ids = ids.astype(F32)
+                for piece in range(all_tokens // 128):
+                    cols = pl.ds(piece * 128, 128)
+                    order[pl.ds(start, 16), cols] = jnp.where(
+                        dest[:, cols] == ids, 1.0, 0.0
+                    ).astype(BF16)
 
     fill_order(z * tokens, tokens)
 
@@ -379,34 +411,6 @@
                 gx(src).start()
                 gc(src).start()
 
-    lane = lax.broadcasted_iota(jnp.int32, (32, 128), 1)
-    for i in range(n_chunk):
-        hid_copy(i).wait()
-
-        @pl.loop(0, CHUNK // 32)
-        def _(r, i=i):
-            rows = pl.ds(pl.multiple_of(i * CHUNK + r * 32, 32), 32)
-            sums = []
-            for layer in range(3):
-                values = hid[layer, rows, :].astype(F32)
-                sums.append(jnp.sum(values * values, axis=-1, keepdims=True))
-            sqcol[rows, :] = jnp.where(
-                lane == 0, sums[0], jnp.where(lane == 1, sums[1], sums[2])
-            )
-
-    sqsend[...] = sqcol[...].T[:8]
-
-    def sq(k):
-        return send(
-            sqsend,
-            sqrecv.at[k - 1],
-            sq_ss.at[k - 1],
-            sq_rs.at[k - 1],
-            {"tensor": (t + k) % N_TP},
-        )
-
-    for k in range(1, N_TP):
-        sq(k).start()
     for k in range(1, N_TP):
         sq(k).wait_recv()
     total = sqsend[...] + sqrecv[0] + sqrecv[1] + sqrecv[2]
@@ -430,27 +434,32 @@
         )
 
     for i in range(n_chunk):
-        for k in (1, 2, 3, 0):
-            cols = lanes(zto(k), feats)
-
-            @pl.loop(0, CHUNK // 16)
-            def _(r, i=i, k=k, cols=cols):
-                rows = pl.ds(pl.multiple_of(i * CHUNK + r * 16, 16), 16)
-                factors = invcol[rows, :]
-                mixture = jnp.zeros((16, feats), F32)
-                for layer in range(3):
-                    scaled = hid[layer, rows, cols].astype(F32) * gain_ref[pl.ds(layer, 1), cols]
-                    mixture = mixture + scaled * factors[:, layer : layer + 1]
-                if k:
-                    jloc[k - 1, rows, :] = mixture.astype(BF16)
-                else:
-                    mine = pl.ds(pl.multiple_of(z * tokens + i * CHUNK + r * 16, 16), 16)
-                    jfeat[mine, :] = mixture.astype(BF16)
-
-            if k:
-                jsend(k, i).start()
-        if i:
-            relay(i)
+
+        @pl.loop(0, CHUNK // 16)
+        def _(r, i=i):
+            rows = pl.ds(pl.multiple_of(i * CHUNK + r * 16, 16), 16)
+            mine = pl.ds(pl.multiple_of(z * tokens + i * CHUNK + r * 16, 16), 16)
+            table = invcol[rows, :]
+            factors = [
+                jnp.broadcast_to(table[:, layer : layer + 1], (16, 128)) for layer in range(3)
+            ]
+            for k in range(N_DP):
+                for piece in range(feats // 128):
+                    cols = pl.ds(pl.multiple_of(zto(k) * feats + piece * 128, 128), 128)
+                    mixture = jnp.zeros((16, 128), F32)
+                    for layer in range(3):
+                        scaled = hid[layer, rows, cols].astype(F32) * gain_ref[layer : layer + 1, cols]
+                        mixture = mixture + scaled * factors[layer]
+                    out = pl.ds(piece * 128, 128)
+                    if k:
+                        jloc[k - 1, rows, out] = mixture.astype(BF16)
+                    else:
+                        jfeat[mine, out] = mixture.astype(BF16)
+
+        for k in range(1, N_DP):
+            jsend(k, i).start()
+        if i == 2:
+            relay(1)
 
     n_unit = N_DP * n_chunk
 
@@ -503,6 +512,12 @@
         def _():
             project(step)
 
+        for hop in (2, 3):
+
+            @pl.when(step == 5 * hop + 2)
+            def _(hop=hop):
+                relay(hop)
+
         @pl.when((step >= 1) & (step <= n_unit))
         def _():
             along_x(step - 1)
@@ -564,10 +579,6 @@
                 ksend[o] = (kpart[o] + krecv[side, o].astype(F32)).astype(BF16)
                 kz(side, o).start()
 
-    for d in range(N_DP):
-        gx_arrived(d).wait_recv()
-        gxc(d).start()
-
     @pl.loop(0, 2 * N_DP)
     def _(b):
         rows = pl.ds(pl.multiple_of(b * (tokens // 2), tokens // 2), tokens // 2)
@@ -575,18 +586,24 @@
             order[rows, :], jfeat[...], preferred_element_type=F32
         ).astype(BF16)
 
+    stage(0)
+
     @pl.loop(0, N_DP * n_chunk)
     def _(b):
         block = pl.ds(pl.multiple_of(b * CHUNK, CHUNK), CHUNK)
         jturn[:, block] = jown[block, :].T
 
-    stage(0)
+    stage(1)
+    for d in range(N_DP):
+        gx_arrived(d).wait_recv()
+        gxc(d).start()
+
     for k in range(N_DP):
         gc_arrived(k, t_c).wait_recv()
         gc_arrived(4 + k, t_xc).wait_recv()
     for n in range(N_TP):
         if n == 2:
-            stage(1)
+            stage(2)
         cols = pl.ds(n * share, share)
 
         @pl.loop(0, feats // CHUNK)
@@ -600,8 +617,6 @@
                     preferred_element_type=F32,
                 )
             wgrad_ref[rows, cols] = value
-
-    stage(2)
 
     @pl.when(z > 0)
     def _():

time: 148 us -> 120 us (0.81)
  the two profiles are of different devices: /device:TPU:20 before, /device:TPU:9 now
where the time goes in v3:
time: 120 us
  Pallas kernels  114 us (95%)
  local copies, waits for them, and re-layouts  5.22 us (4%)
    pallas_call x1, Pallas kernels, fused(): pl.pallas_call(fused_kernel, out_shape=(jax.ShapeDtypeStruct((3, tokens,...  114 us
    unnamed x2, local copies, waits for them, and re-layouts  5.22 us

profile of v3, /device:TPU:9, one launch (start us, length us, event | category | flops | bytes accessed | tf_op | source)
XLA Modules:
  0.0 119.9 jit_solution(8009686586257585134)
XLA Ops:
  0.6 114.0 %draft_head.1 = (bf16[3,512,256]{2,1,0:T(8,128)(2,1)}, f32[512,1024]{1,0:T(8,128)}) custom-call(s32[1,128]{1,0:T(1,128)} %bitcast.13, s32[1,128]{1,0:T(1,128)} %bitcast.14, s32[1,128]{1,0:T(1,128)} %bitcast.15, s32[1,2048]{1,0:T(1,128)} %bitcast.11, bf16[3,512,2048]{2,1,0:T(8,128)(2,1)} %bitcast.9, f32[3,2048]{1,0:T(4,128)} %gain_ref.1, ...), custom_call_target="tpu_custom_call" | custom-call | flops 4294967296 | bytes 12582912 | tf_op jit(solution)/shard_map/draft_head/pallas_call | solution.py:690
  114.6 2.1 %copy.13 = bf16[3,32,16,256]{3,2,1,0:T(8,128)(2,1)} copy(bf16[3,32,16,256]{3,2,1,0:T(8,128)(2,1)} %bitcast.8) | data formatting | bytes 1572864
  116.7 3.2 %copy.14 = f32[512,1024]{1,0:T(8,128)} copy(f32[512,1024]{1,0:T(8,128)} %get-tuple-element.9) | data formatting | bytes 4194304
